TPU v7x, 128 devices: a whole 4x4x4 slice. The times are simulated.
128 devices in a mesh: seq: 8 (over z, core), tensor: 16 (over y, x).
Axes of the slice: x: 4, y: 4, z: 4, core: 2. Of those that a mesh axis runs over, the one named last changes fastest.
Arguments:
- tokens: bfloat16 [6144, 8192], P('seq', 'tensor'), may hold values from -6 to 6
- cotangent: bfloat16 [6144, 10240], P('seq', 'tensor'), may hold values from -6 to 6
- gates: float32 [6144, 4], P('seq'), may hold values from 0.25 to 1
- weight: bfloat16 [8192, 10240], P(None, 'tensor'), may hold values from -0.09375 to 0.09375
- adapter_down_store: bfloat16 [1024, 16, 8192], P('seq', None, 'tensor'), may hold values from -0.0625 to 0.0625
- adapter_up_store: bfloat16 [1024, 16, 10240], P('seq', None, 'tensor'), may hold values from -1.5 to 1.5
- expert_per_group: int32 [8, 4], replicated, may hold values from 0 to 1023, as said below
- adapter_store_row: int32 [1024], replicated, may hold values from 0 to 1023, as said below
Outputs:
- projected: bfloat16 [6144, 10240], P('seq', 'tensor')
- grad_tokens: bfloat16 [6144, 8192], P('seq', 'tensor')
Inputs may be any that keep to these rules, and one draw needn't show every extreme that they name: `expert_per_group`: each row names 4 different adapters; at most 2 of a row's adapters have adapter_store_row // 128 equal, and some row has exactly 2 so. `adapter_store_row`: A permutation of the adapters.
All inputs are finite; a program needn't handle non-finite values.
Results may differ from a plain program's by a relative error of at most 0.004.
Values may be sent and summed in bfloat16 or wider, within the bound.
A program may use at most 192 MiB of HBM per device.

v0:
```python
import jax
import jax.numpy as jnp
from jax import lax
from jax.sharding import PartitionSpec as P

CAP = 2


def per_device(
    tokens,
    cotangent,
    gates,
    weight,
    adapter_down_store,
    adapter_up_store,
    expert_per_group,
    adapter_store_row,
):
    member = lax.axis_index("seq")
    expert_rows = adapter_down_store.shape[0]
    count = expert_per_group.shape[1]
    rows_all = jnp.take(adapter_store_row, expert_per_group, axis=0)
    holders = rows_all // expert_rows
    local_rows = rows_all % expert_rows
    order = jnp.arange(count)
    earlier = (holders[:, :, None] == holders[:, None, :]) & (
        order[None, None, :] < order[None, :, None]
    )
    ranks = jnp.sum(earlier.astype(jnp.int32), axis=2)
    slot_index = jnp.arange(CAP)
    picked = (holders[:, None, :] == member) & (ranks[:, None, :] == slot_index[None, :, None])
    source_device = jnp.sum(jnp.where(picked, local_rows[:, None, :], 0), axis=2)
    filled_slots = jnp.any(picked, axis=2)
    send_down = jnp.where(
        filled_slots[:, :, None, None],
        adapter_down_store[source_device],
        jnp.zeros((), adapter_down_store.dtype),
    )
    outgoing_up = jnp.where(
        filled_slots[:, :, None, None],
        adapter_up_store[source_device],
        jnp.zeros((), adapter_up_store.dtype),
    )
    got_down, got_up = (
        lax.all_to_all(send_down, "seq", split_axis=0, concat_axis=0, tiled=True),
        lax.all_to_all(outgoing_up, "seq", split_axis=0, concat_axis=0, tiled=True),
    )
    mine_holders = lax.dynamic_index_in_dim(holders, member, 0, keepdims=False)
    mine_ranks = lax.dynamic_index_in_dim(ranks, member, 0, keepdims=False)
    flat = mine_holders * CAP + mine_ranks
    down_matrix = got_down.reshape((-1,) + got_down.shape[2:])[flat]
    upper_matrix = got_up.reshape((-1,) + got_up.shape[2:])[flat]
    low_part = jnp.einsum("td,jrd->tjr", tokens, down_matrix, preferred_element_type=jnp.float32)
    back_part = jnp.einsum(
        "tc,jrc->tjr", cotangent, upper_matrix, preferred_element_type=jnp.float32
    )
    low = lax.psum(low_part, "tensor")
    back = lax.psum(back_part, "tensor")
    base = jnp.dot(
        lax.all_gather(tokens, "tensor", axis=1, tiled=True),
        weight,
        preferred_element_type=jnp.float32,
    )
    low_gated = (low * gates[:, :, None]).astype(jnp.bfloat16)
    projected = (
        base
        + jnp.einsum("tjr,jrc->tc", low_gated, upper_matrix, preferred_element_type=jnp.float32)
    ).astype(jnp.bfloat16)
    back_gated = (back * gates[:, :, None]).astype(jnp.bfloat16)
    adapter_grad = jnp.einsum(
        "tjr,jrd->td", back_gated, down_matrix, preferred_element_type=jnp.float32
    )
    partial_grad = lax.dot_general(
        cotangent, weight, (((1,), (1,)), ((), ())), preferred_element_type=jnp.float32
    )
    base_grad = lax.psum_scatter(partial_grad, "tensor", scatter_dimension=1, tiled=True)
    grad_tokens = (base_grad + adapter_grad).astype(jnp.bfloat16)
    return (projected, grad_tokens)


def solution(mesh):
    in_specs = (
        P("seq", "tensor"),
        P("seq", "tensor"),
        P("seq", None),
        P(None, "tensor"),
        P("seq", None, "tensor"),
        P("seq", None, "tensor"),
        P(),
        P(),
    )
    out_specs = (P("seq", "tensor"), P("seq", "tensor"))
    return jax.shard_map(
        per_device, mesh=mesh, in_specs=in_specs, out_specs=out_specs, check_vma=False
    )
```

profile of v0, /device:TPU:0, one launch (start us, length us, event | category | flops | bytes accessed | tf_op | source)
XLA Modules:
  0.0 392.2 jit_solution(12767933084350132623)
XLA Ops:
  7.2 0.8 compare_select_fusion
  8.2 1.4 gather_fusion
  9.8 0.7 add_select_fusion
  10.5 0.7 broadcast_compare_fusion
  11.6 2.2 gather_fusion.1
  13.7 0.8 broadcast_select_fusion.1
  14.5 5.4 %all-to-all-start = ((bf16[8,2,16,512]{3,2,1,0:T(8,128)(2,1)}), bf16[8,2,16,512]{3,2,1,0:T(8,128)(2,1)S(1)}, u32[]{:S(2)}, u32[]{:S(2)}) async-start(bf16[8,2,16,512]{3,2,1,0:T(8,128)(2,1)} %broadcast_select_fusion.1), calls=%async_computation | async-start | bytes 524288 | tf_op jit(solution)/shard_map/all_to_all | solution.py:45
  19.9 0.6 gather_fusion.3
  20.6 0.8 broadcast_select_fusion
  21.6 5.9 %all-to-all-done = bf16[8,2,16,512]{3,2,1,0:T(8,128)(2,1)S(1)} async-done(((bf16[8,2,16,512]{3,2,1,0:T(8,128)(2,1)}), bf16[8,2,16,512]{3,2,1,0:T(8,128)(2,1)S(1)}, u32[]{:S(2)}, u32[]{:S(2)}) %all-to-all-start) | async-done | bytes 262176 | tf_op jit(solution)/shard_map/all_to_all | solution.py:45
  27.5 3.4 all-to-all-start.1
  31.0 0.6 gather_fusion.2
  31.5 2.2 convolution_bitcast_fusion.1
  33.7 5.4 %all-to-all-done.1 = bf16[8,2,16,640]{3,2,1,0:T(8,128)(2,1)S(1)} async-done(((bf16[8,2,16,640]{3,2,1,0:T(8,128)(2,1)}), bf16[8,2,16,640]{3,2,1,0:T(8,128)(2,1)S(1)}, u32[]{:S(2)}, u32[]{:S(2)}) %all-to-all-start.1) | async-done | bytes 327712 | tf_op jit(solution)/shard_map/all_to_all | solution.py:46
  39.1 0.6 gather_fusion.4
  39.6 2.3 convolution_bitcast_fusion
  42.0 0.7 all-gather.2.cloned.1.call-update
  42.8 17.4 %fusion.11 = f32[768,8192]{1,0:T(8,128)} fusion(bf16[768,640]{1,0:T(8,128)(2,1)} %param.9, bf16[8192,640]{1,0:T(8,128)(2,1)} %param.11), kind=kOutput, calls=%fused_computation.44 | convolution fusion | flops 8053063680 | bytes 36634624 | tf_op jit(solution)/shard_map/dot_general | solution.py:73
  60.2 65.6 %all-reduce.3.cloned.1.call-done = (f32[768,4,16]{0,2,1:T(8,128)}, f32[768,4,16]{0,2,1:T(8,128)}) async-done(((f32[768,4,16]{0,2,1:T(8,128)}, f32[768,4,16]{0,2,1:T(8,128)}), (f32[768,4,16]{0,2,1:T(8,128)}, f32[768,4,16]{0,2,1:T(8,128)})) %all-reduce.3.cloned.1.call-update) | async-done | bytes 393232 | tf_op jit(solution)/shard_map/psum | solution.py:57
  125.8 2.6 fusion.4
  128.5 98.5 %all-gather.2.cloned.1.call-done = bf16[768,8192]{1,0:T(8,128)(2,1)} async-done(((bf16[768,512]{1,0:T(8,128)(2,1)}), bf16[768,8192]{1,0:T(8,128)(2,1)}) %all-gather.2.cloned.1.call-update) | async-done | bytes 12582928 | tf_op jit(solution)/shard_map/all_gather | solution.py:60
  226.9 16.0 %fusion = bf16[768,640]{1,0:T(8,128)(2,1)} fusion(f32[768,640,1]{1,0,2:T(8,128)} %fusion.4, bf16[768,8192]{1,0:T(8,128)(2,1)} %all-gather.2.cloned.1.call-done, bf16[8192,640]{1,0:T(8,128)(2,1)} %param.11), kind=kOutput, calls=%fused_computation.6 | convolution fusion | flops 8054046720 | bytes 26017792 | tf_op jit(solution)/shard_map/dot_general | solution.py:59
  242.9 140.1 %reduce-scatter.2.cloned.1.call-done = f32[768,512]{1,0:T(8,128)} async-done(((f32[768,8192]{1,0:T(8,128)}), f32[768,512]{1,0:T(8,128)}) %reduce-scatter.2.cloned.1.call-update) | async-done | bytes 1572880 | tf_op jit(solution)/shard_map/reduce_scatter | solution.py:76
  383.0 2.7 fusion.1
  (28 shorter events, 1.1 us)
Async XLA Ops:
  7.2 12.8 %copy-start = (bf16[128,16,640]{2,1,0:T(8,128)(2,1)S(1)}, bf16[128,16,640]{2,1,0:T(8,128)(2,1)}, u32[]{:S(2)}) copy-start(bf16[128,16,640]{2,1,0:T(8,128)(2,1)} %param.13) | copy-start | bytes 7864324
  14.5 12.9 %all-to-all-start = ((bf16[8,2,16,512]{3,2,1,0:T(8,128)(2,1)}), bf16[8,2,16,512]{3,2,1,0:T(8,128)(2,1)S(1)}, u32[]{:S(2)}, u32[]{:S(2)}) async-start(bf16[8,2,16,512]{3,2,1,0:T(8,128)(2,1)} %broadcast_select_fusion.1), calls=%async_computation | async-start | bytes 524288 | tf_op jit(solution)/shard_map/all_to_all | solution.py:45
  27.5 11.6 %all-to-all-start.1 = ((bf16[8,2,16,640]{3,2,1,0:T(8,128)(2,1)}), bf16[8,2,16,640]{3,2,1,0:T(8,128)(2,1)S(1)}, u32[]{:S(2)}, u32[]{:S(2)}) async-start(bf16[8,2,16,640]{3,2,1,0:T(8,128)(2,1)} %broadcast_select_fusion), calls=%async_computation.1 | async-start | bytes 655360 | tf_op jit(solution)/shard_map/all_to_all | solution.py:46
  30.9 94.9 %all-reduce.3.cloned.1.call-start = ((), (), s32[]{:S(2)}) async-start(), calls=%async_computation.5 | async-start | bytes 786432 | tf_op jit(solution)/shard_map/psum | solution.py:57
  42.0 184.9 %all-gather.2.cloned.1.call-start = ((), (), s32[]{:S(2)}) async-start(), calls=%async_computation.3 | async-start | bytes 13369344 | tf_op jit(solution)/shard_map/all_gather | solution.py:60
  42.7 340.3 %reduce-scatter.2.cloned.1.call-start = ((), (), s32[]{:S(2)}) async-start(), calls=%async_computation.4 | async-start | bytes 26738688 | tf_op jit(solution)/shard_map/reduce_scatter | solution.py:76
  60.2 65.6 %copy-start.2 = (f32[768,4]{0,1:T(4,128)S(1)}, f32[768,4]{0,1:T(4,128)}, u32[]{:S(2)}) copy-start(f32[768,4]{0,1:T(4,128)} %param.10) | copy-start | bytes 36868
  128.5 254.5 %copy-start.1 = (f32[768,4,16]{0,2,1:T(8,128)S(1)}, f32[768,4,16]{0,2,1:T(8,128)}, u32[]{:S(2)}) copy-start(f32[768,4,16]{0,2,1:T(8,128)} %get-tuple-element.3) | copy-start | bytes 589828
Sparse Core Ops, SparseCore 0:
  42.1 83.6 all-reduce.2
  127.9 98.9 all-gather.1
  230.4 152.5 reduce-scatter.1
where the time goes:
time: 394 us; the launch traced here: 392 us
  waiting for transfers between devices  316 us (80%)
  matrix products  43.3 us (11%)
  between operations  13.8 us (4%)
  starting transfers between devices  8.95 us (2%)
  local copies, waits for them, and re-layouts  5.88 us (1%)
  other arithmetic  4.22 us (1%)
    reduce_scatter x1, waiting for transfers between devices, per_device(): lax.psum_scatter(partial_grad, 'tensor', scatter_dimension=1, tiled=True)  140 us
    all_gather x1, waiting for transfers between devices, per_device(): lax.all_gather(tokens, 'tensor', axis=1, tiled=True)  98.5 us
    psum x1, waiting for transfers between devices, per_device(): low = lax.psum(low_part, 'tensor')  65.6 us
    dot_general x1, matrix products, per_device(): lax.dot_general(cotangent, weight, (((1,), (1,)), ((), ())), preferred_el...  17.4 us
    dot_general x1, matrix products, per_device(): jnp.dot(lax.all_gather(tokens, 'tensor', axis=1, tiled=True), weight, pre...  16 us
  transfers between devices with their start and end apart: 5, of which 5 were waited for; matrix products, arithmetic and copies ran while one was open for 10% of the time, Pallas kernels for 0%

commit v1 on v0

v1 whole, which is shorter than its diff:
```python
import jax
import jax.numpy as jnp
from jax import lax
from jax.experimental import pallas as pl
from jax.experimental.pallas import tpu as pltpu
from jax.sharding import PartitionSpec as P

F32 = jnp.float32
BF16 = jnp.bfloat16
MESH = pl.DeviceIdType.MESH
RING = 4
CORES = 2
GROUP = 768
HALF = GROUP // 2
FEATS = 512
COLS = 640
ROW_FEATS = RING * FEATS
ROW_COLS = RING * COLS
RANK = 16
USED = 4
LOW = USED * RANK
STORED = 128
SEQ = RING * CORES
CAP = 2
PIECE = FEATS // CORES
PART = PIECE // 2
CHUNKS = 3
CHUNK = HALF // CHUNKS
TRANSPOSED = (((1,), (1,)), ((), ()))
N_SEMS = 128


def ds(start, size, align):
    return pl.ds(pl.multiple_of(start, align), size)


def kernel(
    tok, cot, gates, weight, down, up, expert, store_row,
    projected, grad_tokens,
    wg, tok_g, cot_g, gate_v, down_v, up_v, ad_send, ad_recv, dd, uu, low_hl, back_hl,
    y_far, y_plus, y_minus, y_keep, y_own, y_relay, y_in, y_out,
    x_far, x_plus, x_minus, x_keep, x_own, x_relay, x_in, x_out,
    local_sem, send_sem, recv_sem,
):
    seq, ten = lax.axis_index("seq"), lax.axis_index("tensor")
    z, c = seq // CORES, lax.rem(seq, CORES)
    y, x = ten // RING, lax.rem(ten, RING)

    def ring(value, step):
        return lax.rem(value + (step + RING), RING)

    def at_x(step):
        return (seq, y * RING + ring(x, step))

    def at_y(step):
        return (seq, ring(y, step) * RING + x)

    def at_z(step):
        return (ring(z, step) * CORES + c, ten)

    other_core = (z * CORES + (1 - c), ten)

    def at_seq(step):
        return (lax.rem(seq + step, SEQ), ten)

    barrier = pltpu.get_barrier_semaphore()
    partners = [at_x(s) for s in (1, 2, 3)] + [at_y(s) for s in (1, 2, 3)]
    partners += [at_seq(s) for s in range(1, SEQ)]
    for partner in partners:
        pl.semaphore_signal(barrier, inc=1, device_id=partner, device_id_type=MESH)

    rows_y = ds(y * ROW_FEATS, ROW_FEATS, ROW_FEATS)
    cols_x = ds(x * FEATS, FEATS, 128)
    cols_y = ds(y * COLS, COLS, 128)
    loads = [
        (down, down_v), (up, up_v), (gates, gate_v),
        (tok, tok_g.at[:, cols_x]), (cot, cot_g.at[:, cols_y]),
        (weight.at[rows_y, :], wg.at[:, cols_y]),
    ]
    loads = [pltpu.make_async_copy(s, d, local_sem.at[i]) for i, (s, d) in enumerate(loads)]
    for load in loads:
        load.start()

    started = []
    names = {}

    def remote(name, src, dst, device):
        i = names.setdefault(name, len(names))
        copy = pltpu.make_async_remote_copy(
            src_ref=src, dst_ref=dst, send_sem=send_sem.at[i], recv_sem=recv_sem.at[i],
            device_id=device, device_id_type=MESH,
        )
        copy.start()
        started.append(copy)
        return copy

    pl.semaphore_wait(barrier, len(partners))

    my_rows = ds(z * FEATS + c * PIECE, PIECE, PIECE)
    w_in = {}
    for step in (2, 1, 3):
        first = ring(y, step) * ROW_FEATS + z * FEATS + c * PIECE
        w_in[step] = remote(
            ("w", step), weight.at[ds(first, PIECE, PIECE), :], wg.at[my_rows, cols_y], at_y(step)
        )

    H = (pl.ds(0, HALF), pl.ds(HALF, HALF))

    def gather_first(name, src, dst, cols, at):
        return (
            remote((name, "p0"), src.at[H[0], :], dst.at[H[0], cols], at(1)),
            remote((name, "m1"), src.at[H[1], :], dst.at[H[1], cols], at(-1)),
        )

    def gather_second(name, src, dst, cols, at):
        return (
            remote((name, "p1"), src.at[H[1], :], dst.at[H[1], cols], at(1)),
            remote((name, "m0"), src.at[H[0], :], dst.at[H[0], cols], at(-1)),
        )

    def gather_relay(name, first, dst, pos, width, at):
        first[0].wait_recv()
        from_left = dst.at[H[0], ds(ring(pos, -1) * width, width, 128)]
        a = remote((name, "r0"), from_left, from_left, at(1))
        first[1].wait_recv()
        from_right = dst.at[H[1], ds(ring(pos, 1) * width, width, 128)]
        b = remote((name, "r1"), from_right, from_right, at(-1))
        return a, b

    tok_first = gather_first("tok", tok, tok_g, cols_x, at_x)
    tok_second = gather_second("tok", tok, tok_g, cols_x, at_x)
    cot_first = gather_first("cot", cot, cot_g, cols_y, at_y)

    loads[0].wait()
    loads[1].wait()

    def fill(g, carry):
        picks = [jnp.int32(0)] * CAP
        count = jnp.int32(0)
        for j in range(USED):
            local = store_row[expert[g, j]] - seq * STORED
            mine = (local >= 0) & (local < STORED)
            for k in range(CAP):
                picks[k] = jnp.where(mine & (count == k), local, picks[k])
            count = count + mine.astype(jnp.int32)
        for k in range(CAP):
            ad_send[g * CAP + k, :, :FEATS] = down_v[picks[k]]
            ad_send[g * CAP + k, :, FEATS:] = up_v[picks[k]]
        return carry

    lax.fori_loop(0, SEQ, fill, 0)
    mine_slots = pl.ds(seq * CAP, CAP)
    ad_in = []
    for step in range(1, SEQ):
        target = at_seq(step)
        ad_in.append(
            remote(("ad", step), ad_send.at[pl.ds(target[0] * CAP, CAP)], ad_recv.at[mine_slots], target)
        )
    for k in range(CAP):
        ad_recv[seq * CAP + k] = ad_send[seq * CAP + k]

    core_in = []

    def to_core(name, place):
        core_in.append((name[1], remote(name, place, place, other_core)))

    def z_place(zz, q, part=None):
        first = zz * FEATS + c * PIECE + (0 if part is None else part * PART)
        return wg.at[ds(first, PIECE if part is None else PART, PART), ds(q * COLS, COLS, 128)]

    def z_start(step):
        w_in[step].wait_recv()
        q = ring(y, -step)
        n = lambda k: ("z", step, k)
        out = {}
        for part in (0, 1):
            here = z_place(z, q, part)
            out["p", part] = remote(n(("p", part)), here, here, at_z(1))
            here = z_place(z, q, 1 - part)
            out["m", 1 - part] = remote(n(("m", 1 - part)), here, here, at_z(-1))
        to_core(("core", step, 0), z_place(z, q))
        return out

    def z_relay(step, out):
        q = ring(y, -step)
        out["p", 0].wait_recv()
        here = z_place(ring(z, -1), q, 0)
        out["r", 0] = remote(("z", step, "r0"), here, here, at_z(1))
        out["m", 1].wait_recv()
        here = z_place(ring(z, 1), q, 1)
        out["r", 1] = remote(("z", step, "r1"), here, here, at_z(-1))

    def z_near(step, out):
        q = ring(y, -step)
        out["p", 1].wait_recv()
        to_core(("core", step, 3), z_place(ring(z, -1), q))
        out["m", 0].wait_recv()
        to_core(("core", step, 1), z_place(ring(z, 1), q))

    def z_far(step, out):
        q = ring(y, -step)
        out["r", 0].wait_recv()
        out["r", 1].wait_recv()
        to_core(("core", step, 2), z_place(ring(z, 2), q))

    def core_wait(step):
        for s, copy in core_in:
            if s == step:
                copy.wait_recv()

    z2 = z_start(2)
    tok_relay = gather_relay("tok", tok_first, tok_g, x, FEATS, at_x)

    for copy in ad_in:
        copy.wait_recv()
    holders = []
    for j in range(USED):
        holder = store_row[expert[seq, j]] // STORED
        rank = jnp.int32(0)
        for earlier in holders:
            rank = rank + (earlier == holder).astype(jnp.int32)
        holders.append(holder)
        rows = ad_recv[holder * CAP + rank]
        dd[pl.ds(j * RANK, RANK), cols_x] = rows[:, :FEATS]
        uu[pl.ds(j * RANK, RANK), cols_y] = rows[:, FEATS:]
    low_rows = pl.ds(0, LOW)
    up_in = []
    down_in = []
    for step in (2, 1, 3):
        here = uu.at[low_rows, cols_y]
        up_in.append(remote(("up", step), here, here, at_y(step)))
        here = dd.at[low_rows, cols_x]
        down_in.append(remote(("down", step), here, here, at_x(step)))
    cot_second = gather_second("cot", cot, cot_g, cols_y, at_y)

    z_relay(2, z2)
    z3 = z_start(3)
    z1 = z_start(1)
    z_near(2, z2)
    z_far(2, z2)

    loads[2].wait()
    lane = lax.broadcasted_iota(jnp.int32, (GROUP, LOW), 1) // RANK
    gate = jnp.zeros((GROUP, LOW), F32)
    for j in range(USED):
        gate = jnp.where(lane == j, gate_v[:, j : j + 1], gate)

    def split_gated(value, out):
        gated = value * gate
        high = gated.astype(BF16)
        out[:, :LOW] = high
        out[:, LOW:] = (gated - high.astype(F32)).astype(BF16)

    for copy in tok_second + tok_relay:
        copy.wait_recv()
    loads[3].wait()
    cot_relay = gather_relay("cot", cot_first, cot_g, y, COLS, at_y)
    for copy in down_in + up_in:
        copy.wait_recv()
    dd[LOW:, :] = dd[:LOW, :]
    uu[LOW:, :] = uu[:LOW, :]
    split_gated(
        lax.dot_general(tok_g[...], dd[:LOW, :], TRANSPOSED, preferred_element_type=F32), low_hl
    )

    def project(q):
        cols = ds(q * COLS, COLS, 128)
        return jnp.dot(tok_g[...], wg[:, cols], preferred_element_type=F32) + jnp.dot(
            low_hl[...], uu[:, cols], preferred_element_type=F32
        )

    def input_grad(q):
        feats = ds(q * FEATS, FEATS, FEATS)
        return lax.dot_general(
            cot_g[...], wg[feats, :], TRANSPOSED, preferred_element_type=F32
        ) + jnp.dot(
            back_hl[...], dd[:, ds(q * FEATS, FEATS, 128)], preferred_element_type=F32
        )

    def far_send(name, value, far, relay, at):
        far[...] = value.astype(BF16)
        return (
            remote((name, "f0"), far.at[H[0], :], relay.at[0], at(1)),
            remote((name, "f1"), far.at[H[1], :], relay.at[1], at(-1)),
        )

    def near_send(name, value, way, out, keep, arrive, at):
        direct = 1 - way
        out[H[direct], :] = value[direct * HALF : (direct + 1) * HALF].astype(BF16)
        copy = remote(
            (name, "n", way), out.at[H[direct], :], arrive.at[way, H[direct], :], at(1 if way == 0 else -1)
        )
        keep[way] = value[way * HALF : (way + 1) * HALF]
        return copy

    def relay_send(name, far_in, way, out, keep, relay, arrive, at):
        far_in[way].wait_recv()
        copies = []
        for k in range(CHUNKS):
            inner = pl.ds(k * CHUNK, CHUNK)
            outer = pl.ds(way * HALF + k * CHUNK, CHUNK)
            out[outer, :] = (keep[way, inner, :] + relay[way, inner, :].astype(F32)).astype(BF16)
            copies.append(
                remote((name, "s", way, k), out.at[outer, :], arrive.at[way, outer, :], at(1 if way == 0 else -1))
            )
        return copies

    def finish(near, sums, own, arrive, out, result, first_sem):
        near[0].wait_recv()
        near[1].wait_recv()
        copies = []
        for k in range(CHUNKS):
            for way in (0, 1):
                sums[way][k].wait_recv()
                rows = pl.ds(way * HALF + k * CHUNK, CHUNK)
                out[rows, :] = (
                    own[rows, :] + arrive[0, rows, :].astype(F32) + arrive[1, rows, :].astype(F32)
                ).astype(BF16)
                copy = pltpu.make_async_copy(
                    out.at[rows, :], result.at[rows, :], local_sem.at[first_sem + len(copies)]
                )
                copy.start()
                copies.append(copy)
        return copies

    core_wait(2)
    loads[5].wait()
    y_far_in = far_send("y", project(ring(y, 2)), y_far, y_relay, at_y)
    z_relay(3, z3)
    y_own[...] = project(y)
    z_near(3, z3)
    z_relay(1, z1)
    z_near(1, z1)
    z_far(3, z3)
    core_wait(3)
    y_near = {}
    z_far(1, z1)
    core_wait(1)
    y_near[0] = near_send("y", project(ring(y, 1)), 0, y_plus, y_keep, y_in, at_y)
    y_near[1] = near_send("y", project(ring(y, -1)), 1, y_minus, y_keep, y_in, at_y)

    for copy in cot_second + cot_relay:
        copy.wait_recv()
    loads[4].wait()
    split_gated(
        lax.dot_general(cot_g[...], uu[:LOW, :], TRANSPOSED, preferred_element_type=F32), back_hl
    )
    x_far_in = far_send("x", input_grad(ring(x, 2)), x_far, x_relay, at_x)
    x_near = {}
    x_near[0] = near_send("x", input_grad(ring(x, 1)), 0, x_plus, x_keep, x_in, at_x)
    x_near[1] = near_send("x", input_grad(ring(x, -1)), 1, x_minus, x_keep, x_in, at_x)
    x_own[...] = input_grad(x)
    y_sums = [
        relay_send("y", y_far_in, 0, y_plus, y_keep, y_relay, y_in, at_y),
        relay_send("y", y_far_in, 1, y_minus, y_keep, y_relay, y_in, at_y),
    ]
    x_sums = [
        relay_send("x", x_far_in, 0, x_plus, x_keep, x_relay, x_in, at_x),
        relay_send("x", x_far_in, 1, x_minus, x_keep, x_relay, x_in, at_x),
    ]
    last = finish(x_near, x_sums, x_own, x_in, x_out, grad_tokens, len(loads))
    last += finish(y_near, y_sums, y_own, y_in, y_out, projected, len(loads) + 2 * CHUNKS)
    for copy in last:
        copy.wait()
    for copy in started:
        copy.wait_send()


def per_device(tokens, cotangent, gates, weight, down, up, expert, store_row):
    any_space = pl.BlockSpec(memory_space=pl.ANY)
    smem = pl.BlockSpec(memory_space=pltpu.SMEM)

    def ring_scratch(width):
        return [
            pltpu.VMEM((GROUP, width), BF16),
            pltpu.VMEM((GROUP, width), BF16),
            pltpu.VMEM((GROUP, width), BF16),
            pltpu.VMEM((2, HALF, width), F32),
            pltpu.VMEM((GROUP, width), F32),
            pltpu.VMEM((2, HALF, width), BF16),
            pltpu.VMEM((2, GROUP, width), BF16),
            pltpu.VMEM((GROUP, width), BF16),
        ]

    flops = 2 * 2 * GROUP * ROW_FEATS * ROW_COLS
    return pl.pallas_call(
        kernel,
        out_shape=(
            jax.ShapeDtypeStruct((GROUP, COLS), BF16),
            jax.ShapeDtypeStruct((GROUP, FEATS), BF16),
        ),
        in_specs=[any_space] * 6 + [smem] * 2,
        out_specs=(any_space, any_space),
        scratch_shapes=[
            pltpu.VMEM((ROW_FEATS, ROW_COLS), BF16),
            pltpu.VMEM((GROUP, ROW_FEATS), BF16),
            pltpu.VMEM((GROUP, ROW_COLS), BF16),
            pltpu.VMEM((GROUP, USED), F32),
            pltpu.VMEM((STORED, RANK, FEATS), BF16),
            pltpu.VMEM((STORED, RANK, COLS), BF16),
            pltpu.VMEM((SEQ * CAP, RANK, FEATS + COLS), BF16),
            pltpu.VMEM((SEQ * CAP, RANK, FEATS + COLS), BF16),
            pltpu.VMEM((2 * LOW, ROW_FEATS), BF16),
            pltpu.VMEM((2 * LOW, ROW_COLS), BF16),
            pltpu.VMEM((GROUP, 2 * LOW), BF16),
            pltpu.VMEM((GROUP, 2 * LOW), BF16),
        ]
        + ring_scratch(COLS)
        + ring_scratch(FEATS)
        + [
            pltpu.SemaphoreType.DMA((6 + 4 * CHUNKS,)),
            pltpu.SemaphoreType.DMA((N_SEMS,)),
            pltpu.SemaphoreType.DMA((N_SEMS,)),
        ],
        compiler_params=pltpu.CompilerParams(
            collective_id=0, has_side_effects=True, vmem_limit_bytes=60 * 2**20
        ),
        cost_estimate=pl.CostEstimate(flops=flops, bytes_accessed=20 * 2**20, transcendentals=0),
        name="mixture",
    )(tokens, cotangent, gates, weight, down, up, expert, store_row)


def solution(mesh):
    return jax.shard_map(
        per_device,
        mesh=mesh,
        in_specs=(
            P("seq", "tensor"),
            P("seq", "tensor"),
            P("seq", None),
            P(None, "tensor"),
            P("seq", None, "tensor"),
            P("seq", None, "tensor"),
            P(),
            P(),
        ),
        out_specs=(P("seq", "tensor"), P("seq", "tensor")),
        check_vma=False,
    )
```

time: 394 us -> 109 us (0.28)
  waiting for transfers between devices: 316 us -> 0 us
  Pallas kernels: 0 us -> 99.1 us
  matrix products: 43.3 us -> 0 us
  between operations: 13.8 us -> 0.64 us
  starting transfers between devices: 8.95 us -> 0 us
  other arithmetic: 4.22 us -> 0 us
    reduce_scatter x1 -> x0, waiting for transfers between devices: 140 us -> none  [per_device(): lax.psum_scatter(partial_grad, 'tensor', scatter_dimension=1, tiled=True)]
    pallas_call x0 -> x1, Pallas kernels: none -> 99.1 us  [per_device(): pl.pallas_call(kernel, out_shape=(jax.ShapeDtypeStruct((GROUP, COLS), BF1...]
    all_gather x1 -> x0, waiting for transfers between devices: 98.5 us -> none  [per_device(): lax.all_gather(tokens, 'tensor', axis=1, tiled=True)]
    psum x1 -> x0, waiting for transfers between devices: 65.6 us -> none  [per_device(): low = lax.psum(low_part, 'tensor')]
    dot_general x6 -> x0, matrix products: 43.3 us -> none  [the longest x1 17.4 us: per_device(): lax.dot_general(cotangent, weight, (((1,), (1,)), ((), ())), preferred_el...]
    all_to_all x2 -> x0, waiting for transfers between devices: 11.3 us -> none  [the longest x1 5.9 us: per_device(): lax.all_to_all(send_down, 'seq', split_axis=0, concat_axis=0, tiled=True)]
    all_to_all x2 -> x0, starting transfers between devices: 8.83 us -> none  [the longest x1 5.4 us: per_device(): lax.all_to_all(send_down, 'seq', split_axis=0, concat_axis=0, tiled=True)]
    unnamed x6 -> x4, local copies, waits for them, and re-layouts: 0.02 us -> 7.28 us
  transfers between devices with their start and end apart: 5 -> 0, of which waited for: 5 -> 0; matrix products, arithmetic and copies ran while one was open for 10% -> 0% of each run, Pallas kernels for 0% -> 0%
where the time goes in v1:
time: 109 us; the launch traced here: 107 us
  Pallas kernels  99.1 us (91%)
  local copies, waits for them, and re-layouts  7.28 us (7%)
    pallas_call x1, Pallas kernels, per_device(): pl.pallas_call(kernel, out_shape=(jax.ShapeDtypeStruct((GROUP, COLS), BF1...  99.1 us
    unnamed x4, local copies, waits for them, and re-layouts  7.28 us

profile of v1, /device:TPU:0, one launch (start us, length us, event | category | flops | bytes accessed | tf_op | source)
XLA Modules:
  0.0 107.0 jit_solution(670511178501978757)
XLA Ops:
  0.6 1.3 %copy.11.expert = s32[8,4]{1,0:T(8,128)} copy(s32[8,4]{0,1:T(4,128)} %param.14) | data formatting | bytes 256 | tf_op args[6]
  2.0 1.6 %copy.10.gates = f32[768,4]{1,0:T(8,128)} copy(f32[768,4]{0,1:T(4,128)} %param.10) | data formatting | bytes 24576 | tf_op args[2]
  3.6 99.1 %mixture.1 = (bf16[768,640]{1,0:T(8,128)(2,1)}, bf16[768,512]{1,0:T(8,128)(2,1)}) custom-call(bf16[768,512]{1,0:T(8,128)(2,1)} %tok.1, bf16[768,640]{1,0:T(8,128)(2,1)} %cot.1, f32[768,4]{1,0:T(8,128)} %copy.10.gates, bf16[8192,640]{1,0:T(8,128)(2,1)} %weight.1, bf16[128,16,512]{2,1,0:T(8,128)(2,1)} %down.1, bf16[128,16,640]{2,1,0:T(8,128)(2,1)} %up.1, ...), custom_call_target="tpu_custom_call" | custom-call | flops 16106127360 | bytes 20971520 | tf_op jit(solution)/shard_map/mixture/pallas_call | solution.py:386
  102.7 2.2 %copy.14 = bf16[768,640]{1,0:T(8,128)(2,1)} copy(bf16[768,640]{1,0:T(8,128)(2,1)} %get-tuple-element.4) | data formatting | bytes 1966080
  104.9 2.1 %copy.15 = bf16[768,512]{1,0:T(8,128)(2,1)} copy(bf16[768,512]{1,0:T(8,128)(2,1)} %get-tuple-element.5) | data formatting | bytes 1572864

commit v2 on v1

--- a/solution.py
+++ b/solution.py
@@ -28,6 +28,7 @@
 CHUNK = HALF // CHUNKS
 TRANSPOSED = (((1,), (1,)), ((), ()))
 N_SEMS = 128
+COPIES = 4
 
 
 def ds(start, size, align):
@@ -37,7 +38,8 @@
 def kernel(
     tok, cot, gates, weight, down, up, expert, store_row,
     projected, grad_tokens,
-    wg, tok_g, cot_g, gate_v, down_v, up_v, ad_send, ad_recv, dd, uu, low_hl, back_hl,
+    wg, tok_g, cot_g, gate_v, gate_t, gate, down_v, up_v, ad_send, ad_recv, dd, uu, low_hl, back_hl,
+    back_part, x2_part,
     y_far, y_plus, y_minus, y_keep, y_own, y_relay, y_in, y_out,
     x_far, x_plus, x_minus, x_keep, x_own, x_relay, x_in, x_out,
     local_sem, send_sem, recv_sem,
@@ -78,7 +80,7 @@
         (weight.at[rows_y, :], wg.at[:, cols_y]),
     ]
     loads = [pltpu.make_async_copy(s, d, local_sem.at[i]) for i, (s, d) in enumerate(loads)]
-    for load in loads:
+    for load in loads[:2]:
         load.start()
 
     started = []
@@ -104,32 +106,37 @@
             ("w", step), weight.at[ds(first, PIECE, PIECE), :], wg.at[my_rows, cols_y], at_y(step)
         )
 
-    H = (pl.ds(0, HALF), pl.ds(HALF, HALF))
+    def chunk(half, k):
+        return pl.ds(half * HALF + k * CHUNK, CHUNK)
+
+    def gather_own(name, way, half, src, dst, cols, at):
+        return [
+            remote((name, way, half, k), src.at[chunk(half, k), :], dst.at[chunk(half, k), cols], at(1 if way == 0 else -1))
+            for k in range(CHUNKS)
+        ]
 
     def gather_first(name, src, dst, cols, at):
-        return (
-            remote((name, "p0"), src.at[H[0], :], dst.at[H[0], cols], at(1)),
-            remote((name, "m1"), src.at[H[1], :], dst.at[H[1], cols], at(-1)),
-        )
+        return [gather_own(name, way, way, src, dst, cols, at) for way in (0, 1)]
 
     def gather_second(name, src, dst, cols, at):
-        return (
-            remote((name, "p1"), src.at[H[1], :], dst.at[H[1], cols], at(1)),
-            remote((name, "m0"), src.at[H[0], :], dst.at[H[0], cols], at(-1)),
-        )
+        return [gather_own(name, way, 1 - way, src, dst, cols, at) for way in (0, 1)]
 
     def gather_relay(name, first, dst, pos, width, at):
-        first[0].wait_recv()
-        from_left = dst.at[H[0], ds(ring(pos, -1) * width, width, 128)]
-        a = remote((name, "r0"), from_left, from_left, at(1))
-        first[1].wait_recv()
-        from_right = dst.at[H[1], ds(ring(pos, 1) * width, width, 128)]
-        b = remote((name, "r1"), from_right, from_right, at(-1))
-        return a, b
+        copies = []
+        for k in range(CHUNKS):
+            for way in (0, 1):
+                first[way][k].wait_recv()
+                step = 1 if way == 0 else -1
+                here = dst.at[chunk(way, k), ds(ring(pos, -step) * width, width, 128)]
+                copies.append(remote((name, "r", way, k), here, here, at(step)))
+        return copies
 
     tok_first = gather_first("tok", tok, tok_g, cols_x, at_x)
     tok_second = gather_second("tok", tok, tok_g, cols_x, at_x)
     cot_first = gather_first("cot", cot, cot_g, cols_y, at_y)
+
+    for load in loads[2:]:
+        load.start()
 
     loads[0].wait()
     loads[1].wait()
@@ -138,7 +145,7 @@
         picks = [jnp.int32(0)] * CAP
         count = jnp.int32(0)
         for j in range(USED):
-            local = store_row[expert[g, j]] - seq * STORED
+            local = store_row[expert[j, g]] - seq * STORED
             mine = (local >= 0) & (local < STORED)
             for k in range(CAP):
                 picks[k] = jnp.where(mine & (count == k), local, picks[k])
@@ -215,7 +222,7 @@
         copy.wait_recv()
     holders = []
     for j in range(USED):
-        holder = store_row[expert[seq, j]] // STORED
+        holder = store_row[expert[j, seq]] // STORED
         rank = jnp.int32(0)
         for earlier in holders:
             rank = rank + (earlier == holder).astype(jnp.int32)
@@ -240,18 +247,19 @@
     z_far(2, z2)
 
     loads[2].wait()
-    lane = lax.broadcasted_iota(jnp.int32, (GROUP, LOW), 1) // RANK
-    gate = jnp.zeros((GROUP, LOW), F32)
     for j in range(USED):
-        gate = jnp.where(lane == j, gate_v[:, j : j + 1], gate)
+        row = jnp.broadcast_to(gate_v[pl.ds(j, 1), :], (RANK, GROUP))
+        gate_t[pl.ds(j * RANK, RANK), :] = row
+        gate_t[pl.ds(LOW + j * RANK, RANK), :] = row
+    gate[...] = gate_t[...].T
+    first_half = lax.broadcasted_iota(jnp.int32, (GROUP, 2 * LOW), 1) < LOW
 
     def split_gated(value, out):
-        gated = value * gate
-        high = gated.astype(BF16)
-        out[:, :LOW] = high
-        out[:, LOW:] = (gated - high.astype(F32)).astype(BF16)
-
-    for copy in tok_second + tok_relay:
+        gated = value * gate[...]
+        high = gated.astype(BF16).astype(F32)
+        out[...] = jnp.where(first_half, high, gated - high).astype(BF16)
+
+    for copy in tok_second[0] + tok_second[1] + tok_relay:
         copy.wait_recv()
     loads[3].wait()
     cot_relay = gather_relay("cot", cot_first, cot_g, y, COLS, at_y)
@@ -260,7 +268,7 @@
     dd[LOW:, :] = dd[:LOW, :]
     uu[LOW:, :] = uu[:LOW, :]
     split_gated(
-        lax.dot_general(tok_g[...], dd[:LOW, :], TRANSPOSED, preferred_element_type=F32), low_hl
+        lax.dot_general(tok_g[...], dd[...], TRANSPOSED, preferred_element_type=F32), low_hl
     )
 
     def project(q):
@@ -279,49 +287,41 @@
 
     def far_send(name, value, far, relay, at):
         far[...] = value.astype(BF16)
-        return (
-            remote((name, "f0"), far.at[H[0], :], relay.at[0], at(1)),
-            remote((name, "f1"), far.at[H[1], :], relay.at[1], at(-1)),
-        )
+        return [
+            [
+                remote((name, "f", way, k), far.at[chunk(way, k), :], relay.at[way, pl.ds(k * CHUNK, CHUNK), :], at(1 if way == 0 else -1))
+                for k in range(CHUNKS)
+            ]
+            for way in (0, 1)
+        ]
 
     def near_send(name, value, way, out, keep, arrive, at):
         direct = 1 - way
-        out[H[direct], :] = value[direct * HALF : (direct + 1) * HALF].astype(BF16)
-        copy = remote(
-            (name, "n", way), out.at[H[direct], :], arrive.at[way, H[direct], :], at(1 if way == 0 else -1)
-        )
+        out[pl.ds(direct * HALF, HALF), :] = value[direct * HALF : (direct + 1) * HALF].astype(BF16)
+        copies = [
+            remote((name, "n", way, k), out.at[chunk(direct, k), :], arrive.at[way, chunk(direct, k), :], at(1 if way == 0 else -1))
+            for k in range(CHUNKS)
+        ]
         keep[way] = value[way * HALF : (way + 1) * HALF]
+        return copies
+
+    def relay_send(name, far_in, way, k, out, keep, relay, arrive, at):
+        far_in[way][k].wait_recv()
+        inner = pl.ds(k * CHUNK, CHUNK)
+        outer = chunk(way, k)
+        out[outer, :] = (keep[way, inner, :] + relay[way, inner, :].astype(F32)).astype(BF16)
+        return remote((name, "s", way, k), out.at[outer, :], arrive.at[way, outer, :], at(1 if way == 0 else -1))
+
+    def finish(near, sums, way, k, own, arrive, out, result, sem):
+        near[1 - way][k].wait_recv()
+        sums[way][k].wait_recv()
+        rows = chunk(way, k)
+        out[rows, :] = (
+            own[rows, :] + arrive[0, rows, :].astype(F32) + arrive[1, rows, :].astype(F32)
+        ).astype(BF16)
+        copy = pltpu.make_async_copy(out.at[rows, :], result.at[rows, :], local_sem.at[sem])
+        copy.start()
         return copy
-
-    def relay_send(name, far_in, way, out, keep, relay, arrive, at):
-        far_in[way].wait_recv()
-        copies = []
-        for k in range(CHUNKS):
-            inner = pl.ds(k * CHUNK, CHUNK)
-            outer = pl.ds(way * HALF + k * CHUNK, CHUNK)
-            out[outer, :] = (keep[way, inner, :] + relay[way, inner, :].astype(F32)).astype(BF16)
-            copies.append(
-                remote((name, "s", way, k), out.at[outer, :], arrive.at[way, outer, :], at(1 if way == 0 else -1))
-            )
-        return copies
-
-    def finish(near, sums, own, arrive, out, result, first_sem):
-        near[0].wait_recv()
-        near[1].wait_recv()
-        copies = []
-        for k in range(CHUNKS):
-            for way in (0, 1):
-                sums[way][k].wait_recv()
-                rows = pl.ds(way * HALF + k * CHUNK, CHUNK)
-                out[rows, :] = (
-                    own[rows, :] + arrive[0, rows, :].astype(F32) + arrive[1, rows, :].astype(F32)
-                ).astype(BF16)
-                copy = pltpu.make_async_copy(
-                    out.at[rows, :], result.at[rows, :], local_sem.at[first_sem + len(copies)]
-                )
-                copy.start()
-                copies.append(copy)
-        return copies
 
     core_wait(2)
     loads[5].wait()
@@ -332,38 +332,77 @@
     z_relay(1, z1)
     z_near(1, z1)
     z_far(3, z3)
+    z_far(1, z1)
     core_wait(3)
-    y_near = {}
-    z_far(1, z1)
     core_wait(1)
-    y_near[0] = near_send("y", project(ring(y, 1)), 0, y_plus, y_keep, y_in, at_y)
-    y_near[1] = near_send("y", project(ring(y, -1)), 1, y_minus, y_keep, y_in, at_y)
-
-    for copy in cot_second + cot_relay:
+
+    loads[4].wait()
+    for copy in cot_second[0] + cot_second[1]:
         copy.wait_recv()
-    loads[4].wait()
-    split_gated(
-        lax.dot_general(cot_g[...], uu[:LOW, :], TRANSPOSED, preferred_element_type=F32), back_hl
+    x2_feats = ds(ring(x, 2) * FEATS, FEATS, FEATS)
+
+    def back_of(q):
+        cols = ds(q * COLS, COLS, 128)
+        return lax.dot_general(cot_g[:, cols], uu[:, cols], TRANSPOSED, preferred_element_type=F32)
+
+    def x2_of(q):
+        cols = ds(q * COLS, COLS, 128)
+        return lax.dot_general(cot_g[:, cols], wg[x2_feats, cols], TRANSPOSED, preferred_element_type=F32)
+
+    back_part[...] = back_of(y) + back_of(ring(y, 1)) + back_of(ring(y, -1))
+    x2_part[...] = x2_of(y) + x2_of(ring(y, 1)) + x2_of(ring(y, -1))
+
+    y_near = [
+        near_send("y", project(ring(y, 1)), 0, y_plus, y_keep, y_in, at_y),
+        near_send("y", project(ring(y, -1)), 1, y_minus, y_keep, y_in, at_y),
+    ]
+
+    for copy in cot_relay:
+        copy.wait_recv()
+    split_gated(back_part[...] + back_of(ring(y, 2)), back_hl)
+    x2_value = x2_part[...] + x2_of(ring(y, 2)) + jnp.dot(
+        back_hl[...], dd[:, ds(ring(x, 2) * FEATS, FEATS, 128)], preferred_element_type=F32
     )
-    x_far_in = far_send("x", input_grad(ring(x, 2)), x_far, x_relay, at_x)
-    x_near = {}
-    x_near[0] = near_send("x", input_grad(ring(x, 1)), 0, x_plus, x_keep, x_in, at_x)
-    x_near[1] = near_send("x", input_grad(ring(x, -1)), 1, x_minus, x_keep, x_in, at_x)
+    x_far_in = far_send("x", x2_value, x_far, x_relay, at_x)
+    x_near = [
+        near_send("x", input_grad(ring(x, 1)), 0, x_plus, x_keep, x_in, at_x),
+        near_send("x", input_grad(ring(x, -1)), 1, x_minus, x_keep, x_in, at_x),
+    ]
     x_own[...] = input_grad(x)
-    y_sums = [
-        relay_send("y", y_far_in, 0, y_plus, y_keep, y_relay, y_in, at_y),
-        relay_send("y", y_far_in, 1, y_minus, y_keep, y_relay, y_in, at_y),
-    ]
-    x_sums = [
-        relay_send("x", x_far_in, 0, x_plus, x_keep, x_relay, x_in, at_x),
-        relay_send("x", x_far_in, 1, x_minus, x_keep, x_relay, x_in, at_x),
-    ]
-    last = finish(x_near, x_sums, x_own, x_in, x_out, grad_tokens, len(loads))
-    last += finish(y_near, y_sums, y_own, y_in, y_out, projected, len(loads) + 2 * CHUNKS)
+    y_sums, x_sums = ([], []), ([], [])
+    for k in range(CHUNKS):
+        y_sums[0].append(relay_send("y", y_far_in, 0, k, y_plus, y_keep, y_relay, y_in, at_y))
+        y_sums[1].append(relay_send("y", y_far_in, 1, k, y_minus, y_keep, y_relay, y_in, at_y))
+        x_sums[0].append(relay_send("x", x_far_in, 0, k, x_plus, x_keep, x_relay, x_in, at_x))
+        x_sums[1].append(relay_send("x", x_far_in, 1, k, x_minus, x_keep, x_relay, x_in, at_x))
+    last = []
+    for k in range(CHUNKS):
+        for way in (0, 1):
+            last.append(finish(x_near, x_sums, way, k, x_own, x_in, x_out, grad_tokens, len(loads) + len(last)))
+        for way in (0, 1):
+            last.append(finish(y_near, y_sums, way, k, y_own, y_in, y_out, projected, len(loads) + len(last)))
     for copy in last:
         copy.wait()
     for copy in started:
         copy.wait_send()
+
+
+def copy_kernel(a, b, a_out, b_out, a_v, b_v, in_sems, out_sems):
+    pairs = []
+    for i, (src, held, dst) in enumerate(((a, a_v, a_out), (b, b_v, b_out))):
+        for k in range(COPIES):
+            rows = pl.ds(k * (GROUP // COPIES), GROUP // COPIES)
+            pairs.append((
+                pltpu.make_async_copy(src.at[rows, :], held.at[rows, :], in_sems.at[i, k]),
+                pltpu.make_async_copy(held.at[rows, :], dst.at[rows, :], out_sems.at[i, k]),
+            ))
+    for fetch, _ in pairs:
+        fetch.start()
+    for fetch, store in pairs:
+        fetch.wait()
+        store.start()
+    for _, store in pairs:
+        store.wait()
 
 
 def per_device(tokens, cotangent, gates, weight, down, up, expert, store_row):
@@ -383,19 +422,22 @@
         ]
 
     flops = 2 * 2 * GROUP * ROW_FEATS * ROW_COLS
-    return pl.pallas_call(
+    outs = (
+        jax.ShapeDtypeStruct((GROUP, COLS), BF16),
+        jax.ShapeDtypeStruct((GROUP, FEATS), BF16),
+    )
+    result = pl.pallas_call(
         kernel,
-        out_shape=(
-            jax.ShapeDtypeStruct((GROUP, COLS), BF16),
-            jax.ShapeDtypeStruct((GROUP, FEATS), BF16),
-        ),
+        out_shape=outs,
         in_specs=[any_space] * 6 + [smem] * 2,
         out_specs=(any_space, any_space),
         scratch_shapes=[
             pltpu.VMEM((ROW_FEATS, ROW_COLS), BF16),
             pltpu.VMEM((GROUP, ROW_FEATS), BF16),
             pltpu.VMEM((GROUP, ROW_COLS), BF16),
-            pltpu.VMEM((GROUP, USED), F32),
+            pltpu.VMEM((USED, GROUP), F32),
+            pltpu.VMEM((2 * LOW, GROUP), F32),
+            pltpu.VMEM((GROUP, 2 * LOW), F32),
             pltpu.VMEM((STORED, RANK, FEATS), BF16),
             pltpu.VMEM((STORED, RANK, COLS), BF16),
             pltpu.VMEM((SEQ * CAP, RANK, FEATS + COLS), BF16),
@@ -404,6 +446,8 @@
             pltpu.VMEM((2 * LOW, ROW_COLS), BF16),
             pltpu.VMEM((GROUP, 2 * LOW), BF16),
             pltpu.VMEM((GROUP, 2 * LOW), BF16),
+            pltpu.VMEM((GROUP, 2 * LOW), F32),
+            pltpu.VMEM((GROUP, FEATS), F32),
         ]
         + ring_scratch(COLS)
         + ring_scratch(FEATS)
@@ -417,7 +461,21 @@
         ),
         cost_estimate=pl.CostEstimate(flops=flops, bytes_accessed=20 * 2**20, transcendentals=0),
         name="mixture",
-    )(tokens, cotangent, gates, weight, down, up, expert, store_row)
+    )(tokens, cotangent, gates.T, weight, down, up, expert.T, store_row)
+    return pl.pallas_call(
+        copy_kernel,
+        out_shape=outs,
+        in_specs=[any_space] * 2,
+        out_specs=(any_space, any_space),
+        scratch_shapes=[
+            pltpu.VMEM((GROUP, COLS), BF16),
+            pltpu.VMEM((GROUP, FEATS), BF16),
+            pltpu.SemaphoreType.DMA((2, COPIES)),
+            pltpu.SemaphoreType.DMA((2, COPIES)),
+        ],
+        compiler_params=pltpu.CompilerParams(vmem_limit_bytes=60 * 2**20),
+        name="results",
+    )(*result)
 
 
 def solution(mesh):

time: 109 us -> 101 us (0.927)
  local copies, waits for them, and re-layouts: 7.28 us -> 0 us
    unnamed x4 -> x0, local copies, waits for them, and re-layouts: 7.28 us -> none
    pallas_call x1 -> x2, Pallas kernels: 99.1 us -> 98.6 us  [the longest x1 96.2 us: per_device(): pl.pallas_call(kernel, out_shape=outs, in_specs=[any_space] * 6 + [smem]...]
where the time goes in v2:
time: 101 us; the launch traced here: 99.4 us
  Pallas kernels  98.6 us (98%)
    pallas_call x1, Pallas kernels, per_device(): pl.pallas_call(kernel, out_shape=outs, in_specs=[any_space] * 6 + [smem]...  96.2 us
    pallas_call x1, Pallas kernels, per_device(): pl.pallas_call(copy_kernel, out_shape=outs, in_specs=[any_space] * 2, out...  2.4 us

profile of v2, /device:TPU:0, one launch (start us, length us, event | category | flops | bytes accessed | tf_op | source)
XLA Modules:
  0.0 99.4 jit_solution(10364475981946177490)
XLA Ops:
  0.6 96.2 %mixture.1 = (bf16[768,640]{1,0:T(8,128)(2,1)}, bf16[768,512]{1,0:T(8,128)(2,1)}) custom-call(bf16[768,512]{1,0:T(8,128)(2,1)} %tok.1, bf16[768,640]{1,0:T(8,128)(2,1)} %cot.1, f32[4,768]{1,0:T(4,128)} %bitcast.2, bf16[8192,640]{1,0:T(8,128)(2,1)} %weight.1, bf16[128,16,512]{2,1,0:T(8,128)(2,1)} %down.1, bf16[128,16,640]{2,1,0:T(8,128)(2,1)} %up.1, ...), custom_call_target="tpu_custom_call" | custom-call | flops 16106127360 | bytes 20971520 | tf_op jit(solution)/shard_map/mixture/pallas_call | solution.py:429
  96.9 2.4 %results.1 = (bf16[768,640]{1,0:T(8,128)(2,1)}, bf16[768,512]{1,0:T(8,128)(2,1)}) custom-call(bf16[768,640]{1,0:T(8,128)(2,1)} %get-tuple-element.4.a, bf16[768,512]{1,0:T(8,128)(2,1)} %get-tuple-element.5.b), custom_call_target="tpu_custom_call" | custom-call | tf_op jit(solution)/shard_map/results/pallas_call | solution.py:465

commit v3 on v2

--- a/solution.py
+++ b/solution.py
@@ -36,13 +36,13 @@
 
 
 def kernel(
-    tok, cot, gates, weight, down, up, expert, store_row,
+    tok, cot, gates, weight, down, up, expert_in, store_row_in,
     projected, grad_tokens,
     wg, tok_g, cot_g, gate_v, gate_t, gate, down_v, up_v, ad_send, ad_recv, dd, uu, low_hl, back_hl,
     back_part, x2_part,
     y_far, y_plus, y_minus, y_keep, y_own, y_relay, y_in, y_out,
     x_far, x_plus, x_minus, x_keep, x_own, x_relay, x_in, x_out,
-    local_sem, send_sem, recv_sem,
+    expert, store_row, local_sem, send_sem, recv_sem,
 ):
     seq, ten = lax.axis_index("seq"), lax.axis_index("tensor")
     z, c = seq // CORES, lax.rem(seq, CORES)
@@ -77,10 +77,10 @@
     loads = [
         (down, down_v), (up, up_v), (gates, gate_v),
         (tok, tok_g.at[:, cols_x]), (cot, cot_g.at[:, cols_y]),
-        (weight.at[rows_y, :], wg.at[:, cols_y]),
+        (weight.at[rows_y, :], wg.at[:, cols_y]), (expert_in, expert), (store_row_in, store_row),
     ]
     loads = [pltpu.make_async_copy(s, d, local_sem.at[i]) for i, (s, d) in enumerate(loads)]
-    for load in loads[:2]:
+    for load in loads[6:] + loads[:2]:
         load.start()
 
     started = []
@@ -135,11 +135,11 @@
     tok_second = gather_second("tok", tok, tok_g, cols_x, at_x)
     cot_first = gather_first("cot", cot, cot_g, cols_y, at_y)
 
-    for load in loads[2:]:
+    for load in loads[2:6]:
         load.start()
 
-    loads[0].wait()
-    loads[1].wait()
+    for load in loads[6:] + loads[:2]:
+        load.wait()
 
     def fill(g, carry):
         picks = [jnp.int32(0)] * CAP
@@ -295,15 +295,17 @@
             for way in (0, 1)
         ]
 
-    def near_send(name, value, way, out, keep, arrive, at):
+    def near_compute(value, way, out, keep):
         direct = 1 - way
         out[pl.ds(direct * HALF, HALF), :] = value[direct * HALF : (direct + 1) * HALF].astype(BF16)
-        copies = [
-            remote((name, "n", way, k), out.at[chunk(direct, k), :], arrive.at[way, chunk(direct, k), :], at(1 if way == 0 else -1))
+        keep[way] = value[way * HALF : (way + 1) * HALF]
+
+    def near_send(name, way, out, arrive, at):
+        rows = [chunk(1 - way, k) for k in range(CHUNKS)]
+        return [
+            remote((name, "n", way, k), out.at[rows[k], :], arrive.at[way, rows[k], :], at(1 if way == 0 else -1))
             for k in range(CHUNKS)
         ]
-        keep[way] = value[way * HALF : (way + 1) * HALF]
-        return copies
 
     def relay_send(name, far_in, way, k, out, keep, relay, arrive, at):
         far_in[way][k].wait_recv()
@@ -323,6 +325,16 @@
         copy.start()
         return copy
 
+    x2_feats = ds(ring(x, 2) * FEATS, FEATS, FEATS)
+
+    def back_of(q):
+        cols = ds(q * COLS, COLS, 128)
+        return lax.dot_general(cot_g[:, cols], uu[:, cols], TRANSPOSED, preferred_element_type=F32)
+
+    def x2_of(q):
+        cols = ds(q * COLS, COLS, 128)
+        return lax.dot_general(cot_g[:, cols], wg[x2_feats, cols], TRANSPOSED, preferred_element_type=F32)
+
     core_wait(2)
     loads[5].wait()
     y_far_in = far_send("y", project(ring(y, 2)), y_far, y_relay, at_y)
@@ -330,32 +342,19 @@
     y_own[...] = project(y)
     z_near(3, z3)
     z_relay(1, z1)
+    loads[4].wait()
+    x2_part[...] = x2_of(y)
+    z_far(3, z3)
     z_near(1, z1)
-    z_far(3, z3)
     z_far(1, z1)
     core_wait(3)
-    core_wait(1)
-
-    loads[4].wait()
     for copy in cot_second[0] + cot_second[1]:
         copy.wait_recv()
-    x2_feats = ds(ring(x, 2) * FEATS, FEATS, FEATS)
-
-    def back_of(q):
-        cols = ds(q * COLS, COLS, 128)
-        return lax.dot_general(cot_g[:, cols], uu[:, cols], TRANSPOSED, preferred_element_type=F32)
-
-    def x2_of(q):
-        cols = ds(q * COLS, COLS, 128)
-        return lax.dot_general(cot_g[:, cols], wg[x2_feats, cols], TRANSPOSED, preferred_element_type=F32)
-
     back_part[...] = back_of(y) + back_of(ring(y, 1)) + back_of(ring(y, -1))
-    x2_part[...] = x2_of(y) + x2_of(ring(y, 1)) + x2_of(ring(y, -1))
-
-    y_near = [
-        near_send("y", project(ring(y, 1)), 0, y_plus, y_keep, y_in, at_y),
-        near_send("y", project(ring(y, -1)), 1, y_minus, y_keep, y_in, at_y),
-    ]
+    x2_part[...] += x2_of(ring(y, 1))
+    core_wait(1)
+    x2_part[...] += x2_of(ring(y, -1))
+    near_compute(project(ring(y, 1)), 0, y_plus, y_keep)
 
     for copy in cot_relay:
         copy.wait_recv()
@@ -364,10 +363,13 @@
         back_hl[...], dd[:, ds(ring(x, 2) * FEATS, FEATS, 128)], preferred_element_type=F32
     )
     x_far_in = far_send("x", x2_value, x_far, x_relay, at_x)
-    x_near = [
-        near_send("x", input_grad(ring(x, 1)), 0, x_plus, x_keep, x_in, at_x),
-        near_send("x", input_grad(ring(x, -1)), 1, x_minus, x_keep, x_in, at_x),
-    ]
+    y_near = [near_send("y", 0, y_plus, y_in, at_y)]
+    near_compute(project(ring(y, -1)), 1, y_minus, y_keep)
+    y_near.append(near_send("y", 1, y_minus, y_in, at_y))
+    near_compute(input_grad(ring(x, 1)), 0, x_plus, x_keep)
+    x_near = [near_send("x", 0, x_plus, x_in, at_x)]
+    near_compute(input_grad(ring(x, -1)), 1, x_minus, x_keep)
+    x_near.append(near_send("x", 1, x_minus, x_in, at_x))
     x_own[...] = input_grad(x)
     y_sums, x_sums = ([], []), ([], [])
     for k in range(CHUNKS):
@@ -407,7 +409,6 @@
 
 def per_device(tokens, cotangent, gates, weight, down, up, expert, store_row):
     any_space = pl.BlockSpec(memory_space=pl.ANY)
-    smem = pl.BlockSpec(memory_space=pltpu.SMEM)
 
     def ring_scratch(width):
         return [
@@ -429,7 +430,7 @@
     result = pl.pallas_call(
         kernel,
         out_shape=outs,
-        in_specs=[any_space] * 6 + [smem] * 2,
+        in_specs=[any_space] * 8,
         out_specs=(any_space, any_space),
         scratch_shapes=[
             pltpu.VMEM((ROW_FEATS, ROW_COLS), BF16),
@@ -452,7 +453,9 @@
         + ring_scratch(COLS)
         + ring_scratch(FEATS)
         + [
-            pltpu.SemaphoreType.DMA((6 + 4 * CHUNKS,)),
+            pltpu.SMEM((USED, SEQ), jnp.int32),
+            pltpu.SMEM((SEQ * STORED,), jnp.int32),
+            pltpu.SemaphoreType.DMA((8 + 4 * CHUNKS,)),
             pltpu.SemaphoreType.DMA((N_SEMS,)),
             pltpu.SemaphoreType.DMA((N_SEMS,)),
         ],

time: 101 us -> 98.6 us (0.976); the launches traced: 99.4 us -> 98.4 us
  no operation moved by 1% of the time
where the time goes in v3:
time: 98.6 us; the launch traced here: 98.4 us
  Pallas kernels  97.6 us (99%)
    pallas_call x1, Pallas kernels, per_device(): pl.pallas_call(kernel, out_shape=outs, in_specs=[any_space] * 8, out_spec...  95.2 us
    pallas_call x1, Pallas kernels, per_device(): pl.pallas_call(copy_kernel, out_shape=outs, in_specs=[any_space] * 2, out...  2.4 us

profile of v3, /device:TPU:0, one launch (start us, length us, event | category | flops | bytes accessed | tf_op | source)
XLA Modules:
  0.0 98.4 jit_solution(10948107986182948193)
XLA Ops:
  0.6 95.2 %mixture.1 = (bf16[768,640]{1,0:T(8,128)(2,1)}, bf16[768,512]{1,0:T(8,128)(2,1)}) custom-call(bf16[768,512]{1,0:T(8,128)(2,1)} %tok.1, bf16[768,640]{1,0:T(8,128)(2,1)} %cot.1, f32[4,768]{1,0:T(4,128)} %bitcast.2, bf16[8192,640]{1,0:T(8,128)(2,1)} %weight.1, bf16[128,16,512]{2,1,0:T(8,128)(2,1)} %down.1, bf16[128,16,640]{2,1,0:T(8,128)(2,1)} %up.1, ...), custom_call_target="tpu_custom_call" | custom-call | flops 16106127360 | bytes 20971520 | tf_op jit(solution)/shard_map/mixture/pallas_call | solution.py:430
  95.9 2.4 %results.1 = (bf16[768,640]{1,0:T(8,128)(2,1)}, bf16[768,512]{1,0:T(8,128)(2,1)}) custom-call(bf16[768,640]{1,0:T(8,128)(2,1)} %get-tuple-element.4.a, bf16[768,512]{1,0:T(8,128)(2,1)} %get-tuple-element.5.b), custom_call_target="tpu_custom_call" | custom-call | tf_op jit(solution)/shard_map/results/pallas_call | solution.py:468

commit v4 on v3

--- a/solution.py
+++ b/solution.py
@@ -1,3 +1,5 @@
+import math
+
 import jax
 import jax.numpy as jnp
 from jax import lax
@@ -27,8 +29,9 @@
 CHUNKS = 3
 CHUNK = HALF // CHUNKS
 TRANSPOSED = (((1,), (1,)), ((), ()))
-N_SEMS = 128
-COPIES = 4
+N_SEND = 10
+N_RECV = 79
+COPIES = 2
 
 
 def ds(start, size, align):
@@ -83,18 +86,34 @@
     for load in loads[6:] + loads[:2]:
         load.start()
 
-    started = []
-    names = {}
-
-    def remote(name, src, dst, device):
-        i = names.setdefault(name, len(names))
+    send_index, recv_index, sent, received = {}, {}, {}, {}
+
+    def remote(name, src, dst, device, together=None):
+        kind, key = name[0], name if together is None else together
         copy = pltpu.make_async_remote_copy(
-            src_ref=src, dst_ref=dst, send_sem=send_sem.at[i], recv_sem=recv_sem.at[i],
-            device_id=device, device_id_type=MESH,
+            src_ref=src,
+            dst_ref=dst,
+            send_sem=send_sem.at[send_index.setdefault(kind, len(send_index))],
+            recv_sem=recv_sem.at[recv_index.setdefault(key, len(recv_index))],
+            device_id=device,
+            device_id_type=MESH,
         )
         copy.start()
-        started.append(copy)
+        size = math.prod(src.shape)
+        sent[kind] = sent.get(kind, 0) + size
+        received[key] = received.get(key, 0) + size
         return copy
+
+    def wait_for(kind, size, sem):
+        if kind == "ad":
+            whole = ad_send.at[pl.ds(0, size // math.prod(ad_send.shape[1:]))]
+        else:
+            array = tok_g if kind in ("tok", "x", "down") else wg
+            whole = array.at[pl.ds(0, size // array.shape[1]), :]
+        pltpu.make_async_copy(whole, whole, sem).wait()
+
+    def arrived(key):
+        wait_for(key[0], received[key], recv_sem.at[recv_index[key]])
 
     pl.semaphore_wait(barrier, len(partners))
 
@@ -109,9 +128,9 @@
     def chunk(half, k):
         return pl.ds(half * HALF + k * CHUNK, CHUNK)
 
-    def gather_own(name, way, half, src, dst, cols, at):
+    def gather_own(name, way, half, src, dst, cols, at, together=None):
         return [
-            remote((name, way, half, k), src.at[chunk(half, k), :], dst.at[chunk(half, k), cols], at(1 if way == 0 else -1))
+            remote((name, way, half, k), src.at[chunk(half, k), :], dst.at[chunk(half, k), cols], at(1 if way == 0 else -1), together)
             for k in range(CHUNKS)
         ]
 
@@ -119,20 +138,19 @@
         return [gather_own(name, way, way, src, dst, cols, at) for way in (0, 1)]
 
     def gather_second(name, src, dst, cols, at):
-        return [gather_own(name, way, 1 - way, src, dst, cols, at) for way in (0, 1)]
+        for way in (0, 1):
+            gather_own(name, way, 1 - way, src, dst, cols, at, (name, "second"))
 
     def gather_relay(name, first, dst, pos, width, at):
-        copies = []
         for k in range(CHUNKS):
             for way in (0, 1):
                 first[way][k].wait_recv()
                 step = 1 if way == 0 else -1
                 here = dst.at[chunk(way, k), ds(ring(pos, -step) * width, width, 128)]
-                copies.append(remote((name, "r", way, k), here, here, at(step)))
-        return copies
+                remote((name, "r", way, k), here, here, at(step), (name, "relay"))
 
     tok_first = gather_first("tok", tok, tok_g, cols_x, at_x)
-    tok_second = gather_second("tok", tok, tok_g, cols_x, at_x)
+    gather_second("tok", tok, tok_g, cols_x, at_x)
     cot_first = gather_first("cot", cot, cot_g, cols_y, at_y)
 
     for load in loads[2:6]:
@@ -157,19 +175,14 @@
 
     lax.fori_loop(0, SEQ, fill, 0)
     mine_slots = pl.ds(seq * CAP, CAP)
-    ad_in = []
     for step in range(1, SEQ):
         target = at_seq(step)
-        ad_in.append(
-            remote(("ad", step), ad_send.at[pl.ds(target[0] * CAP, CAP)], ad_recv.at[mine_slots], target)
-        )
+        remote(("ad",), ad_send.at[pl.ds(target[0] * CAP, CAP)], ad_recv.at[mine_slots], target)
     for k in range(CAP):
         ad_recv[seq * CAP + k] = ad_send[seq * CAP + k]
 
-    core_in = []
-
-    def to_core(name, place):
-        core_in.append((name[1], remote(name, place, place, other_core)))
+    def to_core(step, place):
+        remote(("core", step), place, place, other_core)
 
     def z_place(zz, q, part=None):
         first = zz * FEATS + c * PIECE + (0 if part is None else part * PART)
@@ -185,7 +198,7 @@
             out["p", part] = remote(n(("p", part)), here, here, at_z(1))
             here = z_place(z, q, 1 - part)
             out["m", 1 - part] = remote(n(("m", 1 - part)), here, here, at_z(-1))
-        to_core(("core", step, 0), z_place(z, q))
+        to_core(step, z_place(z, q))
         return out
 
     def z_relay(step, out):
@@ -200,26 +213,23 @@
     def z_near(step, out):
         q = ring(y, -step)
         out["p", 1].wait_recv()
-        to_core(("core", step, 3), z_place(ring(z, -1), q))
+        to_core(step, z_place(ring(z, -1), q))
         out["m", 0].wait_recv()
-        to_core(("core", step, 1), z_place(ring(z, 1), q))
+        to_core(step, z_place(ring(z, 1), q))
 
     def z_far(step, out):
         q = ring(y, -step)
         out["r", 0].wait_recv()
         out["r", 1].wait_recv()
-        to_core(("core", step, 2), z_place(ring(z, 2), q))
+        to_core(step, z_place(ring(z, 2), q))
 
     def core_wait(step):
-        for s, copy in core_in:
-            if s == step:
-                copy.wait_recv()
+        arrived(("core", step))
 
     z2 = z_start(2)
-    tok_relay = gather_relay("tok", tok_first, tok_g, x, FEATS, at_x)
-
-    for copy in ad_in:
-        copy.wait_recv()
+    gather_relay("tok", tok_first, tok_g, x, FEATS, at_x)
+
+    arrived(("ad",))
     holders = []
     for j in range(USED):
         holder = store_row[expert[j, seq]] // STORED
@@ -231,14 +241,12 @@
         dd[pl.ds(j * RANK, RANK), cols_x] = rows[:, :FEATS]
         uu[pl.ds(j * RANK, RANK), cols_y] = rows[:, FEATS:]
     low_rows = pl.ds(0, LOW)
-    up_in = []
-    down_in = []
     for step in (2, 1, 3):
         here = uu.at[low_rows, cols_y]
-        up_in.append(remote(("up", step), here, here, at_y(step)))
+        remote(("up",), here, here, at_y(step))
         here = dd.at[low_rows, cols_x]
-        down_in.append(remote(("down", step), here, here, at_x(step)))
-    cot_second = gather_second("cot", cot, cot_g, cols_y, at_y)
+        remote(("down",), here, here, at_x(step))
+    gather_second("cot", cot, cot_g, cols_y, at_y)
 
     z_relay(2, z2)
     z3 = z_start(3)
@@ -259,12 +267,12 @@
         high = gated.astype(BF16).astype(F32)
         out[...] = jnp.where(first_half, high, gated - high).astype(BF16)
 
-    for copy in tok_second[0] + tok_second[1] + tok_relay:
-        copy.wait_recv()
+    arrived(("tok", "second"))
+    arrived(("tok", "relay"))
     loads[3].wait()
-    cot_relay = gather_relay("cot", cot_first, cot_g, y, COLS, at_y)
-    for copy in down_in + up_in:
-        copy.wait_recv()
+    gather_relay("cot", cot_first, cot_g, y, COLS, at_y)
+    arrived(("down",))
+    arrived(("up",))
     dd[LOW:, :] = dd[:LOW, :]
     uu[LOW:, :] = uu[:LOW, :]
     split_gated(
@@ -348,16 +356,14 @@
     z_near(1, z1)
     z_far(1, z1)
     core_wait(3)
-    for copy in cot_second[0] + cot_second[1]:
-        copy.wait_recv()
+    arrived(("cot", "second"))
     back_part[...] = back_of(y) + back_of(ring(y, 1)) + back_of(ring(y, -1))
     x2_part[...] += x2_of(ring(y, 1))
     core_wait(1)
     x2_part[...] += x2_of(ring(y, -1))
     near_compute(project(ring(y, 1)), 0, y_plus, y_keep)
 
-    for copy in cot_relay:
-        copy.wait_recv()
+    arrived(("cot", "relay"))
     split_gated(back_part[...] + back_of(ring(y, 2)), back_hl)
     x2_value = x2_part[...] + x2_of(ring(y, 2)) + jnp.dot(
         back_hl[...], dd[:, ds(ring(x, 2) * FEATS, FEATS, 128)], preferred_element_type=F32
@@ -385,8 +391,9 @@
             last.append(finish(y_near, y_sums, way, k, y_own, y_in, y_out, projected, len(loads) + len(last)))
     for copy in last:
         copy.wait()
-    for copy in started:
-        copy.wait_send()
+    for kind, size in sent.items():
+        wait_for(kind, size, send_sem.at[send_index[kind]])
+    assert len(send_index) == N_SEND and len(recv_index) == N_RECV
 
 
 def copy_kernel(a, b, a_out, b_out, a_v, b_v, in_sems, out_sems):
@@ -456,8 +463,8 @@
             pltpu.SMEM((USED, SEQ), jnp.int32),
             pltpu.SMEM((SEQ * STORED,), jnp.int32),
             pltpu.SemaphoreType.DMA((8 + 4 * CHUNKS,)),
-            pltpu.SemaphoreType.DMA((N_SEMS,)),
-            pltpu.SemaphoreType.DMA((N_SEMS,)),
+            pltpu.SemaphoreType.DMA((N_SEND,)),
+            pltpu.SemaphoreType.DMA((N_RECV,)),
         ],
         compiler_params=pltpu.CompilerParams(
             collective_id=0, has_side_effects=True, vmem_limit_bytes=60 * 2**20

time: 98.6 us -> 96.8 us (0.982)
  Pallas kernels: 97.6 us -> 95.9 us
    pallas_call x1, Pallas kernels: 95.2 us -> 93.6 us  [per_device(): pl.pallas_call(kernel, out_shape=outs, in_specs=[any_space] * 8, out_spec...]
where the time goes in v4:
time: 96.8 us; the launch traced here: 96.7 us
  Pallas kernels  95.9 us (99%)
    pallas_call x1, Pallas kernels, per_device(): pl.pallas_call(kernel, out_shape=outs, in_specs=[any_space] * 8, out_spec...  93.6 us
    pallas_call x1, Pallas kernels, per_device(): pl.pallas_call(copy_kernel, out_shape=outs, in_specs=[any_space] * 2, out...  2.3 us

profile of v4, /device:TPU:0, one launch (start us, length us, event | category | flops | bytes accessed | tf_op | source)
XLA Modules:
  0.0 96.7 jit_solution(13518057511923421659)
XLA Ops:
  0.6 93.6 %mixture.1 = (bf16[768,640]{1,0:T(8,128)(2,1)}, bf16[768,512]{1,0:T(8,128)(2,1)}) custom-call(bf16[768,512]{1,0:T(8,128)(2,1)} %tok.1, bf16[768,640]{1,0:T(8,128)(2,1)} %cot.1, f32[4,768]{1,0:T(4,128)} %bitcast.2, bf16[8192,640]{1,0:T(8,128)(2,1)} %weight.1, bf16[128,16,512]{2,1,0:T(8,128)(2,1)} %down.1, bf16[128,16,640]{2,1,0:T(8,128)(2,1)} %up.1, ...), custom_call_target="tpu_custom_call" | custom-call | flops 16106127360 | bytes 20971520 | tf_op jit(solution)/shard_map/mixture/pallas_call | solution.py:437
  94.2 2.3 %results.1 = (bf16[768,640]{1,0:T(8,128)(2,1)}, bf16[768,512]{1,0:T(8,128)(2,1)}) custom-call(bf16[768,640]{1,0:T(8,128)(2,1)} %get-tuple-element.4.a, bf16[768,512]{1,0:T(8,128)(2,1)} %get-tuple-element.5.b), custom_call_target="tpu_custom_call" | custom-call | tf_op jit(solution)/shard_map/results/pallas_call | solution.py:475

commit v5 on v4

--- a/solution.py
+++ b/solution.py
@@ -30,7 +30,7 @@
 CHUNK = HALF // CHUNKS
 TRANSPOSED = (((1,), (1,)), ((), ()))
 N_SEND = 10
-N_RECV = 79
+N_RECV = 67
 COPIES = 2
 
 
@@ -151,7 +151,6 @@
 
     tok_first = gather_first("tok", tok, tok_g, cols_x, at_x)
     gather_second("tok", tok, tok_g, cols_x, at_x)
-    cot_first = gather_first("cot", cot, cot_g, cols_y, at_y)
 
     for load in loads[2:6]:
         load.start()
@@ -195,9 +194,10 @@
         out = {}
         for part in (0, 1):
             here = z_place(z, q, part)
-            out["p", part] = remote(n(("p", part)), here, here, at_z(1))
+            together = None if part == 0 else ("z", step, "near")
+            out["p", part] = remote(n(("p", part)), here, here, at_z(1), together)
             here = z_place(z, q, 1 - part)
-            out["m", 1 - part] = remote(n(("m", 1 - part)), here, here, at_z(-1))
+            out["m", 1 - part] = remote(n(("m", 1 - part)), here, here, at_z(-1), together)
         to_core(step, z_place(z, q))
         return out
 
@@ -205,22 +205,20 @@
         q = ring(y, -step)
         out["p", 0].wait_recv()
         here = z_place(ring(z, -1), q, 0)
-        out["r", 0] = remote(("z", step, "r0"), here, here, at_z(1))
+        remote(("z", step, "far"), here, here, at_z(1))
         out["m", 1].wait_recv()
         here = z_place(ring(z, 1), q, 1)
-        out["r", 1] = remote(("z", step, "r1"), here, here, at_z(-1))
-
-    def z_near(step, out):
+        remote(("z", step, "far"), here, here, at_z(-1))
+
+    def z_near(step):
         q = ring(y, -step)
-        out["p", 1].wait_recv()
+        arrived(("z", step, "near"))
         to_core(step, z_place(ring(z, -1), q))
-        out["m", 0].wait_recv()
         to_core(step, z_place(ring(z, 1), q))
 
-    def z_far(step, out):
+    def z_far(step):
         q = ring(y, -step)
-        out["r", 0].wait_recv()
-        out["r", 1].wait_recv()
+        arrived(("z", step, "far"))
         to_core(step, z_place(ring(z, 2), q))
 
     def core_wait(step):
@@ -241,18 +239,29 @@
         dd[pl.ds(j * RANK, RANK), cols_x] = rows[:, :FEATS]
         uu[pl.ds(j * RANK, RANK), cols_y] = rows[:, FEATS:]
     low_rows = pl.ds(0, LOW)
+    low_half = (pl.ds(0, LOW // 2), pl.ds(LOW // 2, LOW // 2))
+    up_first = []
+    for way in (0, 1):
+        here = uu.at[low_half[way], cols_y]
+        up_first.append(remote(("up", way), here, here, at_y(1 - 2 * way)))
+    for way in (0, 1):
+        here = uu.at[low_half[1 - way], cols_y]
+        remote(("up", "rest"), here, here, at_y(1 - 2 * way))
+    cot_first = gather_first("cot", cot, cot_g, cols_y, at_y)
     for step in (2, 1, 3):
-        here = uu.at[low_rows, cols_y]
-        remote(("up",), here, here, at_y(step))
         here = dd.at[low_rows, cols_x]
         remote(("down",), here, here, at_x(step))
-    gather_second("cot", cot, cot_g, cols_y, at_y)
 
     z_relay(2, z2)
     z3 = z_start(3)
     z1 = z_start(1)
-    z_near(2, z2)
-    z_far(2, z2)
+    for way in (0, 1):
+        up_first[way].wait_recv()
+        here = uu.at[low_half[way], ds(ring(y, 2 * way - 1) * COLS, COLS, 128)]
+        remote(("up", "rest"), here, here, at_y(1 - 2 * way))
+    gather_second("cot", cot, cot_g, cols_y, at_y)
+    z_near(2)
+    z_far(2)
 
     loads[2].wait()
     for j in range(USED):
@@ -272,7 +281,7 @@
     loads[3].wait()
     gather_relay("cot", cot_first, cot_g, y, COLS, at_y)
     arrived(("down",))
-    arrived(("up",))
+    arrived(("up", "rest"))
     dd[LOW:, :] = dd[:LOW, :]
     uu[LOW:, :] = uu[:LOW, :]
     split_gated(
@@ -310,10 +319,8 @@
 
     def near_send(name, way, out, arrive, at):
         rows = [chunk(1 - way, k) for k in range(CHUNKS)]
-        return [
-            remote((name, "n", way, k), out.at[rows[k], :], arrive.at[way, rows[k], :], at(1 if way == 0 else -1))
-            for k in range(CHUNKS)
-        ]
+        for row in rows:
+            remote((name, "n", way), out.at[row, :], arrive.at[way, row, :], at(1 if way == 0 else -1))
 
     def relay_send(name, far_in, way, k, out, keep, relay, arrive, at):
         far_in[way][k].wait_recv()
@@ -322,8 +329,7 @@
         out[outer, :] = (keep[way, inner, :] + relay[way, inner, :].astype(F32)).astype(BF16)
         return remote((name, "s", way, k), out.at[outer, :], arrive.at[way, outer, :], at(1 if way == 0 else -1))
 
-    def finish(near, sums, way, k, own, arrive, out, result, sem):
-        near[1 - way][k].wait_recv()
+    def finish(sums, way, k, own, arrive, out, result, sem):
         sums[way][k].wait_recv()
         rows = chunk(way, k)
         out[rows, :] = (
@@ -348,13 +354,13 @@
     y_far_in = far_send("y", project(ring(y, 2)), y_far, y_relay, at_y)
     z_relay(3, z3)
     y_own[...] = project(y)
-    z_near(3, z3)
+    z_near(3)
     z_relay(1, z1)
     loads[4].wait()
     x2_part[...] = x2_of(y)
-    z_far(3, z3)
-    z_near(1, z1)
-    z_far(1, z1)
+    z_far(3)
+    z_near(1)
+    z_far(1)
     core_wait(3)
     arrived(("cot", "second"))
     back_part[...] = back_of(y) + back_of(ring(y, 1)) + back_of(ring(y, -1))
@@ -369,13 +375,13 @@
         back_hl[...], dd[:, ds(ring(x, 2) * FEATS, FEATS, 128)], preferred_element_type=F32
     )
     x_far_in = far_send("x", x2_value, x_far, x_relay, at_x)
-    y_near = [near_send("y", 0, y_plus, y_in, at_y)]
+    near_send("y", 0, y_plus, y_in, at_y)
     near_compute(project(ring(y, -1)), 1, y_minus, y_keep)
-    y_near.append(near_send("y", 1, y_minus, y_in, at_y))
+    near_send("y", 1, y_minus, y_in, at_y)
     near_compute(input_grad(ring(x, 1)), 0, x_plus, x_keep)
-    x_near = [near_send("x", 0, x_plus, x_in, at_x)]
+    near_send("x", 0, x_plus, x_in, at_x)
     near_compute(input_grad(ring(x, -1)), 1, x_minus, x_keep)
-    x_near.append(near_send("x", 1, x_minus, x_in, at_x))
+    near_send("x", 1, x_minus, x_in, at_x)
     x_own[...] = input_grad(x)
     y_sums, x_sums = ([], []), ([], [])
     for k in range(CHUNKS):
@@ -383,12 +389,15 @@
         y_sums[1].append(relay_send("y", y_far_in, 1, k, y_minus, y_keep, y_relay, y_in, at_y))
         x_sums[0].append(relay_send("x", x_far_in, 0, k, x_plus, x_keep, x_relay, x_in, at_x))
         x_sums[1].append(relay_send("x", x_far_in, 1, k, x_minus, x_keep, x_relay, x_in, at_x))
+    for name in ("x", "y"):
+        for way in (0, 1):
+            arrived((name, "n", way))
     last = []
     for k in range(CHUNKS):
         for way in (0, 1):
-            last.append(finish(x_near, x_sums, way, k, x_own, x_in, x_out, grad_tokens, len(loads) + len(last)))
+            last.append(finish(x_sums, way, k, x_own, x_in, x_out, grad_tokens, len(loads) + len(last)))
         for way in (0, 1):
-            last.append(finish(y_near, y_sums, way, k, y_own, y_in, y_out, projected, len(loads) + len(last)))
+            last.append(finish(y_sums, way, k, y_own, y_in, y_out, projected, len(loads) + len(last)))
     for copy in last:
         copy.wait()
     for kind, size in sent.items():

time: 96.8 us -> 95.8 us (0.990)
  Pallas kernels: 95.9 us -> 94.9 us
    pallas_call x1, Pallas kernels: 93.6 us -> 92.6 us  [per_device(): pl.pallas_call(kernel, out_shape=outs, in_specs=[any_space] * 8, out_spec...]
where the time goes in v5:
time: 95.8 us; the launch traced here: 95.7 us
  Pallas kernels  94.9 us (99%)
    pallas_call x1, Pallas kernels, per_device(): pl.pallas_call(kernel, out_shape=outs, in_specs=[any_space] * 8, out_spec...  92.6 us
    pallas_call x1, Pallas kernels, per_device(): pl.pallas_call(copy_kernel, out_shape=outs, in_specs=[any_space] * 2, out...  2.3 us

profile of v5, /device:TPU:0, one launch (start us, length us, event | category | flops | bytes accessed | tf_op | source)
XLA Modules:
  0.0 95.7 jit_solution(614677156238812519)
XLA Ops:
  0.6 92.6 %mixture.1 = (bf16[768,640]{1,0:T(8,128)(2,1)}, bf16[768,512]{1,0:T(8,128)(2,1)}) custom-call(bf16[768,512]{1,0:T(8,128)(2,1)} %tok.1, bf16[768,640]{1,0:T(8,128)(2,1)} %cot.1, f32[4,768]{1,0:T(4,128)} %bitcast.2, bf16[8192,640]{1,0:T(8,128)(2,1)} %weight.1, bf16[128,16,512]{2,1,0:T(8,128)(2,1)} %down.1, bf16[128,16,640]{2,1,0:T(8,128)(2,1)} %up.1, ...), custom_call_target="tpu_custom_call" | custom-call | flops 16106127360 | bytes 20971520 | tf_op jit(solution)/shard_map/mixture/pallas_call | solution.py:446
  93.2 2.3 %results.1 = (bf16[768,640]{1,0:T(8,128)(2,1)}, bf16[768,512]{1,0:T(8,128)(2,1)}) custom-call(bf16[768,640]{1,0:T(8,128)(2,1)} %get-tuple-element.4.a, bf16[768,512]{1,0:T(8,128)(2,1)} %get-tuple-element.5.b), custom_call_target="tpu_custom_call" | custom-call | tf_op jit(solution)/shard_map/results/pallas_call | solution.py:484

commit v6 on v5

--- a/solution.py
+++ b/solution.py
@@ -28,9 +28,10 @@
 PART = PIECE // 2
 CHUNKS = 3
 CHUNK = HALF // CHUNKS
+SUMS = ((0, CHUNK), (CHUNK, CHUNK), (2 * CHUNK, CHUNK * 3 // 4), (2 * CHUNK + CHUNK * 3 // 4, CHUNK // 4))
 TRANSPOSED = (((1,), (1,)), ((), ()))
 N_SEND = 10
-N_RECV = 67
+N_RECV = 71
 COPIES = 2
 
 
@@ -323,15 +324,18 @@
             remote((name, "n", way), out.at[row, :], arrive.at[way, row, :], at(1 if way == 0 else -1))
 
     def relay_send(name, far_in, way, k, out, keep, relay, arrive, at):
-        far_in[way][k].wait_recv()
-        inner = pl.ds(k * CHUNK, CHUNK)
-        outer = chunk(way, k)
+        first, size = SUMS[k]
+        if first % CHUNK == 0:
+            far_in[way][first // CHUNK].wait_recv()
+        inner = pl.ds(first, size)
+        outer = pl.ds(way * HALF + first, size)
         out[outer, :] = (keep[way, inner, :] + relay[way, inner, :].astype(F32)).astype(BF16)
         return remote((name, "s", way, k), out.at[outer, :], arrive.at[way, outer, :], at(1 if way == 0 else -1))
 
     def finish(sums, way, k, own, arrive, out, result, sem):
         sums[way][k].wait_recv()
-        rows = chunk(way, k)
+        first, size = SUMS[k]
+        rows = pl.ds(way * HALF + first, size)
         out[rows, :] = (
             own[rows, :] + arrive[0, rows, :].astype(F32) + arrive[1, rows, :].astype(F32)
         ).astype(BF16)
@@ -384,7 +388,7 @@
     near_send("x", 1, x_minus, x_in, at_x)
     x_own[...] = input_grad(x)
     y_sums, x_sums = ([], []), ([], [])
-    for k in range(CHUNKS):
+    for k in range(len(SUMS)):
         y_sums[0].append(relay_send("y", y_far_in, 0, k, y_plus, y_keep, y_relay, y_in, at_y))
         y_sums[1].append(relay_send("y", y_far_in, 1, k, y_minus, y_keep, y_relay, y_in, at_y))
         x_sums[0].append(relay_send("x", x_far_in, 0, k, x_plus, x_keep, x_relay, x_in, at_x))
@@ -393,7 +397,7 @@
         for way in (0, 1):
             arrived((name, "n", way))
     last = []
-    for k in range(CHUNKS):
+    for k in range(len(SUMS)):
         for way in (0, 1):
             last.append(finish(x_sums, way, k, x_own, x_in, x_out, grad_tokens, len(loads) + len(last)))
         for way in (0, 1):
@@ -471,7 +475,7 @@
         + [
             pltpu.SMEM((USED, SEQ), jnp.int32),
             pltpu.SMEM((SEQ * STORED,), jnp.int32),
-            pltpu.SemaphoreType.DMA((8 + 4 * CHUNKS,)),
+            pltpu.SemaphoreType.DMA((8 + 4 * len(SUMS),)),
             pltpu.SemaphoreType.DMA((N_SEND,)),
             pltpu.SemaphoreType.DMA((N_RECV,)),
         ],

time: 95.8 us -> 95.7 us (level)
  no operation moved by 1% of the time
where the time goes in v6:
time: 95.7 us; the launch traced here: 95.6 us
  Pallas kernels  94.8 us (99%)
    pallas_call x1, Pallas kernels, per_device(): pl.pallas_call(kernel, out_shape=outs, in_specs=[any_space] * 8, out_spec...  92.5 us
    pallas_call x1, Pallas kernels, per_device(): pl.pallas_call(copy_kernel, out_shape=outs, in_specs=[any_space] * 2, out...  2.3 us

profile of v6, /device:TPU:0, one launch (start us, length us, event | category | flops | bytes accessed | tf_op | source)
XLA Modules:
  0.0 95.6 jit_solution(4366595608216944134)
XLA Ops:
  0.6 92.5 %mixture.1 = (bf16[768,640]{1,0:T(8,128)(2,1)}, bf16[768,512]{1,0:T(8,128)(2,1)}) custom-call(bf16[768,512]{1,0:T(8,128)(2,1)} %tok.1, bf16[768,640]{1,0:T(8,128)(2,1)} %cot.1, f32[4,768]{1,0:T(4,128)} %bitcast.2, bf16[8192,640]{1,0:T(8,128)(2,1)} %weight.1, bf16[128,16,512]{2,1,0:T(8,128)(2,1)} %down.1, bf16[128,16,640]{2,1,0:T(8,128)(2,1)} %up.1, ...), custom_call_target="tpu_custom_call" | custom-call | flops 16106127360 | bytes 20971520 | tf_op jit(solution)/shard_map/mixture/pallas_call | solution.py:450
  93.1 2.3 %results.1 = (bf16[768,640]{1,0:T(8,128)(2,1)}, bf16[768,512]{1,0:T(8,128)(2,1)}) custom-call(bf16[768,640]{1,0:T(8,128)(2,1)} %get-tuple-element.4.a, bf16[768,512]{1,0:T(8,128)(2,1)} %get-tuple-element.5.b), custom_call_target="tpu_custom_call" | custom-call | tf_op jit(solution)/shard_map/results/pallas_call | solution.py:488
